TPU v7x, 32 devices: a whole 2x2x4 slice. The times are simulated.
32 devices in a mesh: dp: 8 (over z, x), rows: 4 (over y, core).
Axes of the slice: x: 2, y: 2, z: 4, core: 2. Of those that a mesh axis runs over, the one named last changes fastest.
Arguments:
- older_output: bfloat16 [1920, 12, 2048], P(('dp', 'rows')), parts along dimension 0, may hold values from -6 to 6
- newer_output: bfloat16 [1920, 12, 2048], P(('dp', 'rows')), parts along dimension 0, may hold values from -6 to 6
- output_grad: bfloat16 [1920, 12, 2048], P(('dp', 'rows')), parts along dimension 0, may hold values from -6 to 6
- older_weight: bfloat16 [2048, 512], P('rows'), may hold values from -0.1875 to 0.1875
- newer_weight: bfloat16 [2048, 512], P('rows'), may hold values from -0.1875 to 0.1875
- square_point: bfloat16 [512, 512], P('rows'), may hold values from -0.25 to 0.25
- column_point: bfloat16 [512, 512], P('rows'), may hold values from -0.25 to 0.25
- square_kernel: float32 [3, 3, 512], replicated, may hold values from -2.4 to 2.4
- column_kernel: float32 [7, 512], replicated, may hold values from -2.4 to 2.4
Outputs:
- cell_output: bfloat16 [1920, 12, 2048], P(('dp', 'rows')), parts along dimension 0
- older_grad: bfloat16 [1920, 12, 2048], P(('dp', 'rows')), parts along dimension 0
- newer_grad: bfloat16 [1920, 12, 2048], P(('dp', 'rows')), parts along dimension 0
There are 8 independent parts, one for each index of `dp`. A program takes and returns all parts, laid end to end along the dimension named above; an argument that names none is the same for every part. Nothing has to cross between parts.
All inputs are finite; a program needn't handle non-finite values.
Results may differ from a plain program's by a relative error of at most 0.0057.
Values may be sent and summed in bfloat16 or wider, within the bound.
A program may use at most 128 MiB of HBM per device.

v0:
```python
import jax
import jax.numpy as jnp
from jax import lax
from jax.experimental import pallas as pl
from jax.experimental.pallas import tpu as pltpu
from jax.sharding import PartitionSpec as P

MESH = pl.DeviceIdType.MESH
F32 = jnp.float32
BF16 = jnp.bfloat16
LANES = 128

HEIGHT = 30


def with_halo(block, sides, width):
    for axis, dim in sides:
        count = lax.axis_size(axis)
        forward = [(i, i + 1) for i in range(count - 1)]
        backward = [(target, source) for source, target in forward]
        low = lax.ppermute(
            lax.slice_in_dim(block, block.shape[dim] - width, None, axis=dim), axis, forward
        )
        high = lax.ppermute(lax.slice_in_dim(block, 0, width, axis=dim), axis, backward)
        block = jnp.concatenate([low, block, high], axis=dim)
    return block


def same_image(first_row, local_rows, offset):
    row_ids = jnp.arange(local_rows, dtype=jnp.int32) + first_row
    inside = jnp.floor_divide(row_ids + offset, HEIGHT) == jnp.floor_divide(row_ids, HEIGHT)
    return jnp.where(inside, 1.0, 0.0).astype(jnp.float32)[:, None, None]


def square_taps(padded, kernel, flip, first_row):
    full = jnp.pad(padded, ((0, 0), (1, 1), (0, 0))).astype(jnp.float32)
    height = full.shape[0] - 2
    across = full.shape[1] - 2
    total = jnp.zeros((height, across, full.shape[2]), jnp.float32)
    for i in range(3):
        keep = same_image(first_row, height, (2 - i if flip else i) - 1)
        for j in range(3):
            first = 2 - i if flip else i
            second = 2 - j if flip else j
            total = total + full[first : first + height, second : second + across, :] * (
                kernel[i, j] * keep
            )
    return total


def column_taps(padded, kernel, flip, first_row):
    full = padded.astype(jnp.float32)
    height = full.shape[0] - 6
    total = jnp.zeros((height, full.shape[1], full.shape[2]), jnp.float32)
    for i in range(7):
        first = 6 - i if flip else i
        keep = same_image(first_row, height, first - 3)
        total = total + full[first : first + height, :, :] * (kernel[i] * keep)
    return total


def local(
    older_output,
    newer_output,
    output_grad,
    older_weight,
    newer_weight,
    square_point,
    column_point,
    square_kernel,
    column_kernel,
):
    height, across, channels = older_output.shape
    filters = square_point.shape[1]
    shape_three = (height, across, filters)
    first_row = lax.axis_index("rows") * height
    pool_kernel = jnp.full((3, 3, filters), 1.0 / 9.0, jnp.float32)
    older_flat = older_output.reshape(-1, channels)
    newer_flat = newer_output.reshape(-1, channels)
    older_relu = jnp.maximum(older_flat, 0)
    newer_relu = jnp.maximum(newer_flat, 0)
    older_full, newer_full = (
        lax.all_gather(older_weight, "rows", axis=0, tiled=True),
        lax.all_gather(newer_weight, "rows", axis=0, tiled=True),
    )
    older_sum = jnp.dot(older_relu, older_full, preferred_element_type=jnp.float32)
    newer_sum = jnp.dot(newer_relu, newer_full, preferred_element_type=jnp.float32)
    older_mixed = older_sum.astype(jnp.bfloat16).reshape(shape_three)
    newer_mixed = newer_sum.astype(jnp.bfloat16).reshape(shape_three)
    square_full, column_full = (
        lax.all_gather(square_point, "rows", axis=0, tiled=True),
        lax.all_gather(column_point, "rows", axis=0, tiled=True),
    )
    older_rim = with_halo(older_mixed, (("rows", 0),), 3)
    newer_rim = with_halo(newer_mixed, (("rows", 0),), 1)
    square_pre = (
        square_taps(newer_rim, square_kernel, False, first_row)
        .astype(jnp.bfloat16)
        .reshape(-1, filters)
    )
    column_pre = (
        column_taps(older_rim, column_kernel, False, first_row)
        .astype(jnp.bfloat16)
        .reshape(-1, filters)
    )
    pooled = square_taps(older_rim[2:-2], pool_kernel, False, first_row).reshape(-1, filters)
    square_branch = jnp.dot(square_pre, square_full, preferred_element_type=jnp.float32)
    column_branch = jnp.dot(column_pre, column_full, preferred_element_type=jnp.float32)
    cell_output = jnp.concatenate(
        [
            square_branch,
            column_branch,
            pooled,
            newer_mixed.reshape(-1, filters).astype(jnp.float32),
        ],
        axis=1,
    )
    cell_output = cell_output.astype(jnp.bfloat16).reshape(height, across, 4 * filters)
    grads = output_grad.reshape(-1, 4 * filters)
    grad_square = grads[:, :filters]
    grad_column = grads[:, filters : 2 * filters]
    grad_pool = grads[:, 2 * filters : 3 * filters].reshape(shape_three)
    grad_same = grads[:, 3 * filters :].reshape(shape_three)
    square_back = (
        jnp.dot(grad_square, square_full.T, preferred_element_type=jnp.float32)
        .astype(jnp.bfloat16)
        .reshape(shape_three)
    )
    column_back = (
        jnp.dot(grad_column, column_full.T, preferred_element_type=jnp.float32)
        .astype(jnp.bfloat16)
        .reshape(shape_three)
    )
    column_rim = with_halo(column_back, (("rows", 0),), 3)
    square_rim, pool_rim = (
        with_halo(square_back, (("rows", 0),), 1),
        with_halo(grad_pool, (("rows", 0),), 1),
    )
    newer_back = (
        (square_taps(square_rim, square_kernel, True, first_row) + grad_same.astype(jnp.float32))
        .astype(jnp.bfloat16)
        .reshape(-1, filters)
    )
    older_back = (
        (
            column_taps(column_rim, column_kernel, True, first_row)
            + square_taps(pool_rim, pool_kernel, True, first_row)
        )
        .astype(jnp.bfloat16)
        .reshape(-1, filters)
    )
    older_mask = jnp.where(older_flat > 0, 1.0, 0.0).astype(jnp.float32)
    newer_mask = jnp.where(newer_flat > 0, 1.0, 0.0).astype(jnp.float32)
    older_term = jnp.dot(older_back, older_full.T, preferred_element_type=jnp.float32)
    newer_term = jnp.dot(newer_back, newer_full.T, preferred_element_type=jnp.float32)
    older_grad = (older_term * older_mask).astype(jnp.bfloat16).reshape(older_output.shape)
    newer_grad = (newer_term * newer_mask).astype(jnp.bfloat16).reshape(newer_output.shape)
    return (cell_output, older_grad, newer_grad)


def round_up(value, step):
    return -(-value // step) * step


def weight_pieces(shards):
    pieces = []
    for index, shard in enumerate(shards):
        half = shard.shape[0] // 2
        rows = min(half, 128)
        pieces += [(index, at, rows) for at in range(0, half, rows)]
    return pieces


class Exchange:
    def __init__(self, shards, fulls, own_sem, y_sems, x_sems, side_sems, pass_sems):
        part, row = lax.axis_index("dp"), lax.axis_index("rows")
        side, across = row + 1 - 2 * (row % 2), (row + 2) % 4
        mate = part + 1 - 2 * (part % 2)
        mine, theirs = part % 2, 1 - part % 2
        barrier = pltpu.get_barrier_semaphore()
        for device in ((part, side), (part, across), (mate, row)):
            pl.semaphore_signal(barrier, inc=1, device_id=device, device_id_type=MESH)
        pl.semaphore_wait(barrier, 3)
        self.pieces = weight_pieces(shards)

        def span(index, owner, half, at, rows):
            depth = shards[index].shape[0]
            return pl.ds(pl.multiple_of(owner * depth + half * (depth // 2) + at, 64), rows)

        def remote(src, dst, sems, slot, device):
            return pltpu.make_async_remote_copy(
                src_ref=src,
                dst_ref=dst,
                send_sem=sems.at[0, slot],
                recv_sem=sems.at[1, slot],
                device_id=device,
                device_id_type=MESH,
            )

        self.y, self.x, self.low, self.high, self.own, self.side = [], [], [], [], [], []
        total = len(self.pieces)
        for slot, (index, at, rows) in enumerate(self.pieces):
            depth = shards[index].shape[0]
            start = pl.ds(pl.multiple_of(mine * (depth // 2) + at, 64), rows)
            sent = fulls[index].at[span(index, row, mine, at, rows)]
            got = fulls[index].at[span(index, across, mine, at, rows)]
            other = fulls[index].at[span(index, across, theirs, at, rows)]
            self.y.append(remote(shards[index].at[start], sent, y_sems, slot, (part, across)))
            self.x.append(remote(got, got, x_sems, slot, (mate, row)))
            self.low.append(remote(got, got, pass_sems, slot, (part, side)))
            self.high.append(remote(other, other, pass_sems, total + slot, (part, side)))
        for index, shard in enumerate(shards):
            depth = shard.shape[0]
            home = fulls[index].at[pl.ds(pl.multiple_of(row * depth, 64), depth)]
            self.side.append(remote(shard, home, side_sems, index, (part, side)))
            self.own.append(pltpu.make_async_copy(shard, home, own_sem.at[index]))
        for copy in self.y + self.side + self.own:
            copy.start()

    def forward(self, slot):
        if slot < len(self.pieces):
            self.y[slot].wait_recv()
            self.x[slot].start()
            self.low[slot].start()
        if slot > 0:
            self.x[slot - 1].wait_recv()
            self.high[slot - 1].start()

    def wait_array(self, index):
        for slot, piece in enumerate(self.pieces):
            if piece[0] == index:
                self.low[slot].wait_recv()
                self.high[slot].wait_recv()
        self.side[index].wait_recv()
        self.own[index].wait()

    def finish(self):
        for copy in self.y + self.x + self.low + self.high + self.side:
            copy.wait_send()


def exchange_semaphores(shards):
    total, number = len(weight_pieces(shards)), len(shards)
    return [
        pltpu.SemaphoreType.DMA((number,)),
        pltpu.SemaphoreType.DMA((2, total)),
        pltpu.SemaphoreType.DMA((2, total)),
        pltpu.SemaphoreType.DMA((2, number)),
        pltpu.SemaphoreType.DMA((2, 2 * total)),
    ]


def dot_rows(left, right):
    return lax.dot_general(left, right, (((1,), (0,)), ((), ())), preferred_element_type=F32)


def dot_turned(left, right):
    return lax.dot_general(left, right, (((1,), (1,)), ((), ())), preferred_element_type=F32)


def make_shift(tall):
    at = lax.broadcasted_iota(jnp.int32, (tall, LANES), 0)
    at = at % HEIGHT
    keeps = {d: (at + d >= 0) & (at + d < HEIGHT) for d in (-3, -2, -1, 1, 2, 3)}

    def shift(value, d):
        return jnp.where(keeps[d], pltpu.roll(value, (-d) % tall, 0), 0.0)

    return shift


def column_sum(value, taps, flip, shift):
    total = value * taps[3]
    for i in (0, 1, 2, 4, 5, 6):
        total = total + shift(value * taps[i], 3 - i if flip else i - 3)
    return total


def square_sum(low, value, high, taps, flip, shift):
    if flip:
        low, high = high, low
    sums = [low * taps[3 * i] + value * taps[3 * i + 1] + high * taps[3 * i + 2] for i in range(3)]
    if flip:
        sums = sums[::-1]
    return sums[1] + shift(sums[0], -1) + shift(sums[2], 1)


def pool_sum(low, value, high, shift):
    total = low + value + high
    return (total + shift(total, -1) + shift(total, 1)) * (1.0 / 9.0)


def lanes(chunk):
    return pl.ds(pl.multiple_of(chunk * LANES, LANES), LANES)


def flat(ref, columns):
    across, tall, _ = ref.shape
    return ref[:, :, columns].reshape(across * tall, columns.size)


def tiles(filters, tile, body):
    @pl.loop(0, filters // tile)
    def _(n):
        body(pl.multiple_of(n * tile, tile))


def planes(first, last, across, body):
    @pl.loop(first, last)
    def _(chunk):
        @pl.loop(0, across)
        def _(w):
            body(w, lanes(chunk))


def tap_rows(ref, columns, number):
    return [ref[pl.ds(i, 1), columns] for i in range(number)]


def clear_ends(rim):
    rim[0] = jnp.zeros(rim.shape[1:], F32)
    rim[rim.shape[0] - 1] = jnp.zeros(rim.shape[1:], F32)


def early_kernel(
    older_hbm,
    grads_hbm,
    square_shard,
    column_shard,
    older_shard,
    square_taps,
    column_taps,
    back_a,
    back_b,
    branch,
    square_hbm,
    older_full_hbm,
    older_in,
    grads_in,
    older_pad,
    grads_pad,
    square_full,
    column_full,
    older_full,
    rim_a,
    rim_b,
    rim_c,
    pre,
    in_sems,
    out_sems,
    *exchange_sems,
):
    across, height, channels = older_in.shape
    tall = older_pad.shape[1]
    filters = square_full.shape[0]
    wide = across * tall
    tile = min(filters, 256)
    chunks = filters // LANES
    ins = [
        pltpu.make_async_copy(grads_hbm, grads_in, in_sems.at[0]),
        pltpu.make_async_copy(older_hbm, older_in, in_sems.at[1]),
    ]
    for copy in ins:
        copy.start()
    trade = Exchange(
        (square_shard, column_shard, older_shard),
        (square_full, column_full, older_full),
        *exchange_sems,
    )
    last = len(trade.pieces)
    clear_ends(rim_a)
    clear_ends(rim_b)
    shift = make_shift(tall)
    ins[0].wait()
    grads_pad[:, :height, :] = grads_in[...]
    trade.forward(0)
    trade.forward(1)
    ins[1].wait()
    older_pad[:, :height, :] = jnp.maximum(older_in[...], 0)
    trade.forward(2)
    trade.wait_array(0)
    trade.wait_array(1)

    def back_tile(at):
        cols = pl.ds(at, tile)
        first = dot_turned(flat(grads_pad, pl.ds(0, filters)), square_full[cols, :])
        rim_a[1 : across + 1, :, cols] = first.astype(BF16).astype(F32).reshape(across, tall, tile)
        second = dot_turned(flat(grads_pad, pl.ds(filters, filters)), column_full[cols, :])
        rim_c[:, :, cols] = second.astype(BF16).astype(F32).reshape(across, tall, tile)
        pool_cols = pl.ds(pl.multiple_of(2 * filters + at, tile), tile)
        rim_b[1 : across + 1, :, cols] = grads_pad[:, :, pool_cols].astype(F32)

    tiles(filters, tile, back_tile)

    def back_plane(w, cols):
        taps = tap_rows(square_taps, cols, 9)
        total = square_sum(rim_a[w, :, cols], rim_a[w + 1, :, cols], rim_a[w + 2, :, cols], taps, True, shift)
        same = pl.ds(pl.multiple_of(3 * filters + cols.start, LANES), LANES)
        back_b[w, :, cols] = (total + grads_pad[w, :, same].astype(F32)).astype(BF16)
        total = column_sum(rim_c[w, :, cols], tap_rows(column_taps, cols, 7), True, shift)
        total = total + pool_sum(rim_b[w, :, cols], rim_b[w + 1, :, cols], rim_b[w + 2, :, cols], shift)
        back_a[w, :, cols] = total.astype(BF16)

    done = 0
    for slot in range(3, last + 1):
        until = (slot - 2) * chunks // max(1, last - 2)
        planes(done, until, across, back_plane)
        done = until
        trade.forward(slot)
    if done < chunks:
        planes(done, chunks, across, back_plane)
    trade.wait_array(2)
    outs = [
        pltpu.make_async_copy(square_full, square_hbm, out_sems.at[0]),
        pltpu.make_async_copy(older_full, older_full_hbm, out_sems.at[1]),
    ]
    for copy in outs:
        copy.start()

    def mix_tile(at):
        cols = pl.ds(at, tile)
        mixed = dot_rows(older_pad[...].reshape(wide, channels), older_full[:, cols])
        rim_b[1 : across + 1, :, cols] = mixed.astype(BF16).astype(F32).reshape(across, tall, tile)

    tiles(filters, tile, mix_tile)

    def mix_plane(w, cols):
        total = column_sum(rim_b[w + 1, :, cols], tap_rows(column_taps, cols, 7), False, shift)
        pre[w, :, cols] = total.astype(BF16)
        total = pool_sum(rim_b[w, :, cols], rim_b[w + 1, :, cols], rim_b[w + 2, :, cols], shift)
        pool = pl.ds(pl.multiple_of(filters + cols.start, LANES), LANES)
        branch[w, :, pool] = total[:height].astype(BF16)

    planes(0, chunks, across, mix_plane)

    def point_tile(at):
        cols = pl.ds(at, tile)
        term = dot_rows(pre[...].reshape(wide, filters), column_full[:, cols])
        branch[:, :, cols] = term.reshape(across, tall, tile)[:, :height].astype(BF16)

    tiles(filters, tile, point_tile)
    trade.finish()
    for copy in outs:
        copy.wait()


def early(older, grads, square_shard, column_shard, older_shard, square_taps, column_taps, count):
    across, height, channels = older.shape
    filters = square_shard.shape[1]
    tall = round_up(height, 16)
    plain = pltpu.VMEM((across, height, channels), BF16)
    padded = pltpu.VMEM((across, tall, channels), BF16)
    rim = pltpu.VMEM((across + 2, tall, filters), F32)
    shards = (square_shard, column_shard, older_shard)
    fulls = [(count * x.shape[0], x.shape[1]) for x in shards]
    anywhere = pl.BlockSpec(memory_space=pl.ANY)
    inside = pl.BlockSpec(memory_space=pltpu.VMEM)
    back = jax.ShapeDtypeStruct((across, tall, filters), BF16)
    flops = 2 * across * tall * filters * (channels + 3 * filters)
    return pl.pallas_call(
        early_kernel,
        out_shape=[
            back,
            back,
            jax.ShapeDtypeStruct((across, height, 2 * filters), BF16),
            jax.ShapeDtypeStruct(fulls[0], BF16),
            jax.ShapeDtypeStruct(fulls[2], BF16),
        ],
        in_specs=[anywhere] * 5 + [inside] * 2,
        out_specs=[inside] * 3 + [anywhere] * 2,
        scratch_shapes=[plain, plain, padded, padded]
        + [pltpu.VMEM(shape, BF16) for shape in fulls]
        + [rim, rim, pltpu.VMEM((across, tall, filters), F32)]
        + [pltpu.VMEM((across, tall, filters), BF16)]
        + [pltpu.SemaphoreType.DMA((2,)), pltpu.SemaphoreType.DMA((2,))]
        + exchange_semaphores(shards),
        compiler_params=pltpu.CompilerParams(
            collective_id=0, has_side_effects=True, vmem_limit_bytes=48 * 1024 * 1024
        ),
        cost_estimate=pl.CostEstimate(flops=flops, bytes_accessed=20 * older.size, transcendentals=0),
        name="early",
    )(older, grads, *shards, square_taps, column_taps)


def grad_blocks(back, full, pad, buf, hbm, sems, height):
    across, tall, filters = back.shape
    channels = full.shape[0]
    tile = min(filters, 256)
    outs = []
    for q in range(channels // filters):

        def grad_tile(at, base=q * filters):
            cols = pl.ds(pl.multiple_of(base + at, tile), tile)
            term = dot_turned(back[...].reshape(across * tall, filters), full[cols, :])
            term = jnp.where(pad[:, :, cols] > 0, term.reshape(across, tall, tile), 0.0)
            buf[:, :, cols] = term[:, :height].astype(BF16)

        tiles(filters, tile, grad_tile)
        cols = pl.ds(q * filters, filters)
        outs.append(pltpu.make_async_copy(buf.at[:, :, cols], hbm.at[:, :, cols], sems.at[q]))
        outs[-1].start()
    return outs


def older_kernel(older_hbm, back, full, out_hbm, older_in, pad, buf, in_sem, out_sems):
    height = older_in.shape[1]
    load = pltpu.make_async_copy(older_hbm, older_in, in_sem)
    load.start()
    load.wait()
    pad[:, :height, :] = older_in[...]
    for copy in grad_blocks(back, full, pad, buf, out_hbm, out_sems, height):
        copy.wait()


def older_part(older, back, full):
    across, height, channels = older.shape
    tall, filters = back.shape[1:]
    plain = pltpu.VMEM(older.shape, BF16)
    anywhere = pl.BlockSpec(memory_space=pl.ANY)
    inside = pl.BlockSpec(memory_space=pltpu.VMEM)
    return pl.pallas_call(
        older_kernel,
        out_shape=jax.ShapeDtypeStruct(older.shape, BF16),
        in_specs=[anywhere, inside, inside],
        out_specs=anywhere,
        scratch_shapes=[plain, pltpu.VMEM((across, tall, channels), BF16), plain]
        + [pltpu.SemaphoreType.DMA(()), pltpu.SemaphoreType.DMA((channels // filters,))],
        compiler_params=pltpu.CompilerParams(vmem_limit_bytes=40 * 1024 * 1024),
        cost_estimate=pl.CostEstimate(
            flops=2 * across * tall * filters * channels, bytes_accessed=6 * older.size, transcendentals=0
        ),
        name="older",
    )(older, back, full)


def newer_kernel(
    newer_hbm,
    branch_hbm,
    back,
    newer_full,
    square_full,
    square_taps,
    cell_hbm,
    out_hbm,
    newer_in,
    pad,
    buf,
    cell_buf,
    rim,
    pre,
    in_sems,
    out_sems,
    grad_sems,
):
    across, height, channels = newer_in.shape
    tall = pad.shape[1]
    filters = square_full.shape[0]
    wide = across * tall
    tile = min(filters, 256)
    load = pltpu.make_async_copy(newer_hbm, newer_in, in_sems.at[0])
    load.start()
    middle = pl.ds(filters, 2 * filters)
    fetch = pltpu.make_async_copy(branch_hbm, cell_buf.at[:, :, middle], in_sems.at[1])
    fetch.start()
    clear_ends(rim)
    shift = make_shift(tall)
    load.wait()
    pad[:, :height, :] = jnp.maximum(newer_in[...], 0)
    outs = grad_blocks(back, newer_full, pad, buf, out_hbm, grad_sems, height)
    fetch.wait()

    def send(columns, slot):
        copy = pltpu.make_async_copy(cell_buf.at[:, :, columns], cell_hbm.at[:, :, columns], out_sems.at[slot])
        copy.start()
        outs.append(copy)

    send(middle, 0)

    def mix_tile(at):
        cols = pl.ds(at, tile)
        total = dot_rows(pad[...].reshape(wide, channels), newer_full[:, cols])
        mixed = total.astype(BF16).reshape(across, tall, tile)
        rim[1 : across + 1, :, cols] = mixed.astype(F32)
        cell_buf[:, :, pl.ds(pl.multiple_of(3 * filters + at, tile), tile)] = mixed[:, :height]

    tiles(filters, tile, mix_tile)
    send(pl.ds(3 * filters, filters), 1)

    def mix_plane(w, cols):
        taps = tap_rows(square_taps, cols, 9)
        total = square_sum(rim[w, :, cols], rim[w + 1, :, cols], rim[w + 2, :, cols], taps, False, shift)
        pre[w, :, cols] = total.astype(BF16)

    planes(0, filters // LANES, across, mix_plane)

    def point_tile(at):
        cols = pl.ds(at, tile)
        term = dot_rows(pre[...].reshape(wide, filters), square_full[:, cols])
        cell_buf[:, :, cols] = term.reshape(across, tall, tile)[:, :height].astype(BF16)

    tiles(filters, tile, point_tile)
    send(pl.ds(0, filters), 2)
    for copy in outs:
        copy.wait()


def newer_part(newer, branch, back, newer_full, square_full, square_taps):
    across, height, channels = newer.shape
    tall, filters = back.shape[1:]
    plain = pltpu.VMEM(newer.shape, BF16)
    anywhere = pl.BlockSpec(memory_space=pl.ANY)
    inside = pl.BlockSpec(memory_space=pltpu.VMEM)
    return pl.pallas_call(
        newer_kernel,
        out_shape=[jax.ShapeDtypeStruct(newer.shape, BF16)] * 2,
        in_specs=[anywhere] * 2 + [inside] * 4,
        out_specs=[anywhere] * 2,
        scratch_shapes=[plain, pltpu.VMEM((across, tall, channels), BF16), plain, plain]
        + [pltpu.VMEM((across + 2, tall, filters), F32), pltpu.VMEM((across, tall, filters), BF16)]
        + [pltpu.SemaphoreType.DMA((2,)), pltpu.SemaphoreType.DMA((3,))]
        + [pltpu.SemaphoreType.DMA((channels // filters,))],
        compiler_params=pltpu.CompilerParams(vmem_limit_bytes=48 * 1024 * 1024),
        name="newer",
    )(newer, branch, back, newer_full, square_full, square_taps)


def whole_images(
    older_output,
    newer_output,
    output_grad,
    older_weight,
    newer_weight,
    square_point,
    column_point,
    square_kernel,
    column_kernel,
):
    count = lax.axis_size("rows")
    filters = square_point.shape[1]
    newer_full = lax.all_gather(newer_weight, "rows", axis=0, tiled=True)
    older, newer, grads = (jnp.transpose(x, (1, 0, 2)) for x in (older_output, newer_output, output_grad))
    square_taps = square_kernel.reshape(9, filters)
    back_a, back_b, branch, square_full, older_full = early(
        older, grads, square_point, column_point, older_weight, square_taps, column_kernel, count
    )
    older_grad = older_part(older, back_a, older_full)
    cell_output, newer_grad = newer_part(newer, branch, back_b, newer_full, square_full, square_taps)
    return tuple(jnp.transpose(x, (1, 0, 2)) for x in (cell_output, older_grad, newer_grad))


def choose(*arrays):
    height = arrays[0].shape[0]
    routes = lax.axis_size("rows") == 4 and lax.axis_size("dp") % 2 == 0
    if height % HEIGHT == 0 and routes:
        return whole_images(*arrays)
    return local(*arrays)


def solution(mesh):
    in_specs = (
        P(("dp", "rows"), None, None),
        P(("dp", "rows"), None, None),
        P(("dp", "rows"), None, None),
        P("rows", None),
        P("rows", None),
        P("rows", None),
        P("rows", None),
        P(),
        P(),
    )
    out_specs = (
        P(("dp", "rows"), None, None),
        P(("dp", "rows"), None, None),
        P(("dp", "rows"), None, None),
    )
    return jax.shard_map(choose, mesh=mesh, in_specs=in_specs, out_specs=out_specs, check_vma=False)
```

profile of v0, /device:TPU:0, one launch (start us, length us, event | category | flops | bytes accessed | tf_op | source)
XLA Modules:
  0.0 67.3 jit_solution(9476176355323447302)
XLA Ops:
  7.2 0.0 all-gather.2.cloned.1.call-start
  7.2 0.7 %all-gather.2.cloned.1.call-update = ((bf16[512,512]{1,0:T(8,128)(2,1)}), bf16[2048,512]{1,0:T(8,128)(2,1)}) async-update(((), (), s32[]{:S(2)}) %all-gather.2.cloned.1.call-start, bf16[512,512]{1,0:T(8,128)(2,1)} %param.13) | async-update | bytes 3145752
  7.9 0.8 %reshape.9.square_taps = f32[9,512]{1,0:T(8,128)S(1)} reshape(f32[3,3,512]{2,1,0:T(4,128)} %param.16) | data formatting | bytes 36864 | tf_op jit(solution)/shard_map/reshape | solution.py:642
  8.7 0.0 copy-start.3
  8.7 1.0 %copy-done.3 = bf16[512,512]{1,0:T(8,128)(2,1)S(1)} copy-done((bf16[512,512]{1,0:T(8,128)(2,1)S(1)}, bf16[512,512]{1,0:T(8,128)(2,1)}, u32[]{:S(2)}) %copy-start.3) | copy-done | bytes 524312
  9.7 0.0 copy-start.4
  9.7 0.9 %copy-done.4 = bf16[128,512]{1,0:T(8,128)(2,1)S(1)} copy-done((bf16[128,512]{1,0:T(8,128)(2,1)S(1)}, bf16[128,512]{1,0:T(8,128)(2,1)}, u32[]{:S(2)}) %copy-start.4) | copy-done | bytes 131096
  10.6 0.0 copy-start.5
  10.6 0.9 %copy-done.5 = bf16[128,512]{1,0:T(8,128)(2,1)S(1)} copy-done((bf16[128,512]{1,0:T(8,128)(2,1)S(1)}, bf16[128,512]{1,0:T(8,128)(2,1)}, u32[]{:S(2)}) %copy-start.5) | copy-done | bytes 131096
  11.5 0.0 copy-start.6
  11.5 0.7 %copy-done.6 = f32[7,512]{1,0:T(8,128)S(1)} copy-done((f32[7,512]{1,0:T(8,128)S(1)}, f32[7,512]{1,0:T(8,128)}, u32[]{:S(2)}) %copy-start.6) | copy-done | bytes 14360
  12.2 0.0 copy-start
  12.2 29.5 %early.1 = (bf16[12,64,512]{2,1,0:T(8,128)(2,1)S(1)}, bf16[12,64,512]{2,1,0:T(8,128)(2,1)S(1)}, bf16[12,60,1024]{2,1,0:T(8,128)(2,1)S(1)}, bf16[512,512]{1,0:T(8,128)(2,1)S(1)}, bf16[2048,512]{1,0:T(8,128)(2,1)}) custom-call(bf16[12,60,2048]{2,1,0:T(8,128)(2,1)} %bitcast.6, bf16[12,60,2048]{2,1,0:T(8,128)(2,1)} %bitcast.10, bf16[128,512]{1,0:T(8,128)(2,1)S(1)} %copy-done.4, ...), custom_call_target="tpu_custom_call" | custom-call | flops 2818572288 | bytes 29491200 | tf_op jit(solution)/shard_map/early/pallas_call | solution.py:460
  41.7 0.0 copy-done
  41.7 0.0 copy-start.2
  41.7 1.6 %copy-done.2 = bf16[2048,512]{1,0:T(8,128)(2,1)S(1)} copy-done((bf16[2048,512]{1,0:T(8,128)(2,1)S(1)}, bf16[2048,512]{1,0:T(8,128)(2,1)}, u32[]{:S(2)}) %copy-start.2) | copy-done | bytes 2097176
  43.3 4.5 %older.1 = bf16[12,60,2048]{2,1,0:T(8,128)(2,1)} custom-call(bf16[12,60,2048]{2,1,0:T(8,128)(2,1)S(1)} %bitcast.7, bf16[12,64,512]{2,1,0:T(8,128)(2,1)S(1)} %get-tuple-element.14.back, bf16[2048,512]{1,0:T(8,128)(2,1)S(1)} %copy-done.2), custom_call_target="tpu_custom_call" | custom-call | flops 1610612736 | bytes 8847360 | tf_op jit(solution)/shard_map/older/pallas_call | solution.py:521
  47.9 0.0 all-gather.2.cloned.1.call-done.newer_full
  47.9 0.0 copy-start.1
  47.9 1.6 %copy-done.1 = bf16[2048,512]{1,0:T(8,128)(2,1)S(1)} copy-done((bf16[2048,512]{1,0:T(8,128)(2,1)S(1)}, bf16[2048,512]{1,0:T(8,128)(2,1)}, u32[]{:S(2)}) %copy-start.1) | copy-done | bytes 2097176
  49.5 10.9 %newer.1 = (bf16[12,60,2048]{2,1,0:T(8,128)(2,1)}, bf16[12,60,2048]{2,1,0:T(8,128)(2,1)}) custom-call(bf16[12,60,2048]{2,1,0:T(8,128)(2,1)} %bitcast.9, bf16[12,60,1024]{2,1,0:T(8,128)(2,1)S(1)} %get-tuple-element.10.branch_hbm, bf16[12,64,512]{2,1,0:T(8,128)(2,1)S(1)} %get-tuple-element.11.back, bf16[2048,512]{1,0:T(8,128)(2,1)S(1)} %copy-done.1, ...), custom_call_target="tpu_custom_call" | custom-call | tf_op jit(solution)/shard_map/newer/pallas_call | solution.py:613
Async XLA Ops:
  7.2 40.7 %all-gather.2.cloned.1.call-start = ((), (), s32[]{:S(2)}) async-start(), calls=%async_computation | async-start | bytes 2621440 | tf_op jit(solution)/shard_map/all_gather | solution.py:640
  8.7 1.0 %copy-start.3 = (bf16[512,512]{1,0:T(8,128)(2,1)S(1)}, bf16[512,512]{1,0:T(8,128)(2,1)}, u32[]{:S(2)}) copy-start(bf16[512,512]{1,0:T(8,128)(2,1)} %older_shard.1) | copy-start | bytes 1572868
  9.7 0.9 %copy-start.4 = (bf16[128,512]{1,0:T(8,128)(2,1)S(1)}, bf16[128,512]{1,0:T(8,128)(2,1)}, u32[]{:S(2)}) copy-start(bf16[128,512]{1,0:T(8,128)(2,1)} %square_shard.1) | copy-start | bytes 393220
  10.6 0.9 %copy-start.5 = (bf16[128,512]{1,0:T(8,128)(2,1)S(1)}, bf16[128,512]{1,0:T(8,128)(2,1)}, u32[]{:S(2)}) copy-start(bf16[128,512]{1,0:T(8,128)(2,1)} %column_shard.1) | copy-start | bytes 393220
  11.5 0.7 %copy-start.6 = (f32[7,512]{1,0:T(8,128)S(1)}, f32[7,512]{1,0:T(8,128)}, u32[]{:S(2)}) copy-start(f32[7,512]{1,0:T(8,128)} %column_taps.1) | copy-start | bytes 43012
  12.2 29.5 %copy-start = (bf16[60,12,2048]{2,0,1:T(8,128)(2,1)S(1)}, bf16[60,12,2048]{2,0,1:T(8,128)(2,1)}, u32[]{:S(2)}) copy-start(bf16[60,12,2048]{2,0,1:T(8,128)(2,1)} %param.9) | copy-start | bytes 8847364
  41.7 1.6 %copy-start.2 = (bf16[2048,512]{1,0:T(8,128)(2,1)S(1)}, bf16[2048,512]{1,0:T(8,128)(2,1)}, u32[]{:S(2)}) copy-start(bf16[2048,512]{1,0:T(8,128)(2,1)} %get-tuple-element.15.full) | copy-start | bytes 6291460
  47.9 1.6 %copy-start.1 = (bf16[2048,512]{1,0:T(8,128)(2,1)S(1)}, bf16[2048,512]{1,0:T(8,128)(2,1)}, u32[]{:S(2)}) copy-start(bf16[2048,512]{1,0:T(8,128)(2,1)} %all-gather.2.cloned.1.call-done.newer_full) | copy-start | bytes 6291460
Sparse Core Ops, SparseCore 0:
  9.6 28.6 all-gather.1
where the time goes:
time: 67.7 us; the launch traced here: 67.3 us
  Pallas kernels  45 us (66%)
  between operations  14.1 us (21%)
  local copies, waits for them, and re-layouts  7.48 us (11%)
  waiting for transfers between devices  0.7 us (1%)
    pallas_call x1, Pallas kernels, early(): pl.pallas_call(early_kernel, out_shape=[back, back, jax.ShapeDtypeStruct(...  29.5 us
    pallas_call x1, Pallas kernels, newer_part(): pl.pallas_call(newer_kernel, out_shape=[jax.ShapeDtypeStruct(newer.shape,...  10.9 us
    unnamed x14, local copies, waits for them, and re-layouts  6.73 us
    pallas_call x1, Pallas kernels, older_part(): pl.pallas_call(older_kernel, out_shape=jax.ShapeDtypeStruct(older.shape,...  4.54 us
  transfers between devices with their start and end apart: 1, of which 0 were waited for; matrix products, arithmetic and copies ran while one was open for 1% of the time, Pallas kernels for 51%

commit v1 on v0

--- a/solution.py
+++ b/solution.py
@@ -172,20 +172,17 @@
 
 
 class Exchange:
-    def __init__(self, shards, fulls, own_sem, y_sems, x_sems, side_sems, pass_sems):
+    def __init__(self, shards, fulls, own_sem, y_sems, x_sems, side_sems):
         part, row = lax.axis_index("dp"), lax.axis_index("rows")
         side, across = row + 1 - 2 * (row % 2), (row + 2) % 4
+        corner = across + 1 - 2 * (across % 2)
         mate = part + 1 - 2 * (part % 2)
-        mine, theirs = part % 2, 1 - part % 2
+        mine = part % 2
         barrier = pltpu.get_barrier_semaphore()
-        for device in ((part, side), (part, across), (mate, row)):
+        for device in ((part, side), (part, across), (part, corner), (mate, row)):
             pl.semaphore_signal(barrier, inc=1, device_id=device, device_id_type=MESH)
-        pl.semaphore_wait(barrier, 3)
+        pl.semaphore_wait(barrier, 4)
         self.pieces = weight_pieces(shards)
-
-        def span(index, owner, half, at, rows):
-            depth = shards[index].shape[0]
-            return pl.ds(pl.multiple_of(owner * depth + half * (depth // 2) + at, 64), rows)
 
         def remote(src, dst, sems, slot, device):
             return pltpu.make_async_remote_copy(
@@ -197,45 +194,55 @@
                 device_id_type=MESH,
             )
 
-        self.y, self.x, self.low, self.high, self.own, self.side = [], [], [], [], [], []
-        total = len(self.pieces)
+        self.y, self.x, self.own, self.side = [], [], [], []
         for slot, (index, at, rows) in enumerate(self.pieces):
             depth = shards[index].shape[0]
-            start = pl.ds(pl.multiple_of(mine * (depth // 2) + at, 64), rows)
-            sent = fulls[index].at[span(index, row, mine, at, rows)]
-            got = fulls[index].at[span(index, across, mine, at, rows)]
-            other = fulls[index].at[span(index, across, theirs, at, rows)]
-            self.y.append(remote(shards[index].at[start], sent, y_sems, slot, (part, across)))
-            self.x.append(remote(got, got, x_sems, slot, (mate, row)))
-            self.low.append(remote(got, got, pass_sems, slot, (part, side)))
-            self.high.append(remote(other, other, pass_sems, total + slot, (part, side)))
+            base = mine * (depth // 2) + at
+            start = shards[index].at[pl.ds(pl.multiple_of(base, 64), rows)]
+            sent, near, far = (
+                fulls[index].at[pl.ds(pl.multiple_of(owner * depth + base, 64), rows)]
+                for owner in (row, across, corner)
+            )
+            self.y.append(
+                [
+                    remote(start, sent, y_sems, 2 * slot, (part, across)),
+                    remote(start, sent, y_sems, 2 * slot + 1, (part, corner)),
+                ]
+            )
+            self.x.append(
+                [
+                    remote(near, near, x_sems, 2 * slot, (mate, row)),
+                    remote(far, far, x_sems, 2 * slot + 1, (mate, row)),
+                ]
+            )
         for index, shard in enumerate(shards):
             depth = shard.shape[0]
             home = fulls[index].at[pl.ds(pl.multiple_of(row * depth, 64), depth)]
             self.side.append(remote(shard, home, side_sems, index, (part, side)))
             self.own.append(pltpu.make_async_copy(shard, home, own_sem.at[index]))
-        for copy in self.y + self.side + self.own:
-            copy.start()
+        for index in range(len(shards)):
+            for slot, piece in enumerate(self.pieces):
+                if piece[0] == index:
+                    self.y[slot][0].start()
+                    self.y[slot][1].start()
+            self.side[index].start()
+            self.own[index].start()
 
     def forward(self, slot):
-        if slot < len(self.pieces):
-            self.y[slot].wait_recv()
-            self.x[slot].start()
-            self.low[slot].start()
-        if slot > 0:
-            self.x[slot - 1].wait_recv()
-            self.high[slot - 1].start()
+        for come, go in zip(self.y[slot], self.x[slot]):
+            come.wait_recv()
+            go.start()
 
     def wait_array(self, index):
         for slot, piece in enumerate(self.pieces):
             if piece[0] == index:
-                self.low[slot].wait_recv()
-                self.high[slot].wait_recv()
+                for copy in self.x[slot]:
+                    copy.wait_recv()
         self.side[index].wait_recv()
         self.own[index].wait()
 
     def finish(self):
-        for copy in self.y + self.x + self.low + self.high + self.side:
+        for copy in sum(self.y, []) + sum(self.x, []) + self.side:
             copy.wait_send()
 
 
@@ -243,10 +250,9 @@
     total, number = len(weight_pieces(shards)), len(shards)
     return [
         pltpu.SemaphoreType.DMA((number,)),
-        pltpu.SemaphoreType.DMA((2, total)),
-        pltpu.SemaphoreType.DMA((2, total)),
+        pltpu.SemaphoreType.DMA((2, 2 * total)),
+        pltpu.SemaphoreType.DMA((2, 2 * total)),
         pltpu.SemaphoreType.DMA((2, number)),
-        pltpu.SemaphoreType.DMA((2, 2 * total)),
     ]
 
 
@@ -324,28 +330,37 @@
 
 def early_kernel(
     older_hbm,
+    newer_hbm,
     grads_hbm,
     square_shard,
     column_shard,
     older_shard,
+    newer_shard,
     square_taps,
     column_taps,
-    back_a,
-    back_b,
-    branch,
-    square_hbm,
+    back_a_hbm,
+    back_b_hbm,
+    cell_hbm,
     older_full_hbm,
+    newer_full_hbm,
     older_in,
+    newer_in,
     grads_in,
     older_pad,
+    newer_pad,
     grads_pad,
     square_full,
     column_full,
     older_full,
+    newer_full,
     rim_a,
     rim_b,
     rim_c,
-    pre,
+    pre_a,
+    pre_b,
+    back_a,
+    back_b,
+    cell_buf,
     in_sems,
     out_sems,
     *exchange_sems,
@@ -357,17 +372,28 @@
     tile = min(filters, 256)
     chunks = filters // LANES
     ins = [
-        pltpu.make_async_copy(grads_hbm, grads_in, in_sems.at[0]),
-        pltpu.make_async_copy(older_hbm, older_in, in_sems.at[1]),
+        pltpu.make_async_copy(src, dst, in_sems.at[n])
+        for n, (src, dst) in enumerate(
+            ((grads_hbm, grads_in), (older_hbm, older_in), (newer_hbm, newer_in))
+        )
     ]
+    trade = Exchange(
+        (square_shard, column_shard, older_shard, newer_shard),
+        (square_full, column_full, older_full, newer_full),
+        *exchange_sems,
+    )
     for copy in ins:
         copy.start()
-    trade = Exchange(
-        (square_shard, column_shard, older_shard),
-        (square_full, column_full, older_full),
-        *exchange_sems,
-    )
-    last = len(trade.pieces)
+    outs = []
+
+    def put(src, dst):
+        outs.append(pltpu.make_async_copy(src, dst, out_sems.at[len(outs)]))
+        outs[-1].start()
+
+    def put_block(q):
+        cols = pl.ds(q * filters, filters)
+        put(cell_buf.at[:, :, cols], cell_hbm.at[:, :, cols])
+
     clear_ends(rim_a)
     clear_ends(rim_b)
     shift = make_shift(tall)
@@ -377,7 +403,8 @@
     trade.forward(1)
     ins[1].wait()
     older_pad[:, :height, :] = jnp.maximum(older_in[...], 0)
-    trade.forward(2)
+    ins[2].wait()
+    newer_pad[:, :height, :] = jnp.maximum(newer_in[...], 0)
     trade.wait_array(0)
     trade.wait_array(1)
 
@@ -401,85 +428,112 @@
         total = total + pool_sum(rim_b[w, :, cols], rim_b[w + 1, :, cols], rim_b[w + 2, :, cols], shift)
         back_a[w, :, cols] = total.astype(BF16)
 
+    older_slots = [n for n, piece in enumerate(trade.pieces) if piece[0] == 2]
+    newer_slots = [n for n, piece in enumerate(trade.pieces) if piece[0] == 3]
     done = 0
-    for slot in range(3, last + 1):
-        until = (slot - 2) * chunks // max(1, last - 2)
+    for n, slot in enumerate(older_slots):
+        until = (n + 1) * chunks // len(older_slots)
         planes(done, until, across, back_plane)
         done = until
         trade.forward(slot)
-    if done < chunks:
-        planes(done, chunks, across, back_plane)
+    put(back_a, back_a_hbm)
+    put(back_b, back_b_hbm)
     trade.wait_array(2)
-    outs = [
-        pltpu.make_async_copy(square_full, square_hbm, out_sems.at[0]),
-        pltpu.make_async_copy(older_full, older_full_hbm, out_sems.at[1]),
-    ]
-    for copy in outs:
-        copy.start()
-
-    def mix_tile(at):
+    put(older_full, older_full_hbm)
+
+    def older_tile(at):
         cols = pl.ds(at, tile)
         mixed = dot_rows(older_pad[...].reshape(wide, channels), older_full[:, cols])
         rim_b[1 : across + 1, :, cols] = mixed.astype(BF16).astype(F32).reshape(across, tall, tile)
 
-    tiles(filters, tile, mix_tile)
-
-    def mix_plane(w, cols):
+    tiles(filters, tile, older_tile)
+
+    def older_plane(w, cols):
         total = column_sum(rim_b[w + 1, :, cols], tap_rows(column_taps, cols, 7), False, shift)
-        pre[w, :, cols] = total.astype(BF16)
+        pre_a[w, :, cols] = total.astype(BF16)
         total = pool_sum(rim_b[w, :, cols], rim_b[w + 1, :, cols], rim_b[w + 2, :, cols], shift)
-        pool = pl.ds(pl.multiple_of(filters + cols.start, LANES), LANES)
-        branch[w, :, pool] = total[:height].astype(BF16)
-
-    planes(0, chunks, across, mix_plane)
-
-    def point_tile(at):
+        pool = pl.ds(pl.multiple_of(2 * filters + cols.start, LANES), LANES)
+        cell_buf[w, :, pool] = total[:height].astype(BF16)
+
+    done = 0
+    for n, slot in enumerate(newer_slots):
+        trade.forward(slot)
+        until = (n + 1) * chunks // len(newer_slots)
+        planes(done, until, across, older_plane)
+        done = until
+    put_block(2)
+
+    def point_blocks(q, pre, full):
+        def point_tile(at):
+            term = dot_rows(pre[...].reshape(wide, filters), full[:, pl.ds(at, tile)])
+            cols = pl.ds(pl.multiple_of(q * filters + at, tile), tile)
+            cell_buf[:, :, cols] = term.reshape(across, tall, tile)[:, :height].astype(BF16)
+
+        tiles(filters, tile, point_tile)
+        put_block(q)
+
+    point_blocks(1, pre_a, column_full)
+    trade.wait_array(3)
+    put(newer_full, newer_full_hbm)
+
+    def newer_tile(at):
         cols = pl.ds(at, tile)
-        term = dot_rows(pre[...].reshape(wide, filters), column_full[:, cols])
-        branch[:, :, cols] = term.reshape(across, tall, tile)[:, :height].astype(BF16)
-
-    tiles(filters, tile, point_tile)
+        total = dot_rows(newer_pad[...].reshape(wide, channels), newer_full[:, cols])
+        mixed = total.astype(BF16).reshape(across, tall, tile)
+        rim_a[1 : across + 1, :, cols] = mixed.astype(F32)
+        cell_buf[:, :, pl.ds(pl.multiple_of(3 * filters + at, tile), tile)] = mixed[:, :height]
+
+    tiles(filters, tile, newer_tile)
+    put_block(3)
+
+    def newer_plane(w, cols):
+        taps = tap_rows(square_taps, cols, 9)
+        total = square_sum(rim_a[w, :, cols], rim_a[w + 1, :, cols], rim_a[w + 2, :, cols], taps, False, shift)
+        pre_b[w, :, cols] = total.astype(BF16)
+
+    planes(0, chunks, across, newer_plane)
+    point_blocks(0, pre_b, square_full)
     trade.finish()
     for copy in outs:
         copy.wait()
 
 
-def early(older, grads, square_shard, column_shard, older_shard, square_taps, column_taps, count):
+def early(older, newer, grads, shards, square_taps, column_taps, count):
     across, height, channels = older.shape
-    filters = square_shard.shape[1]
+    filters = shards[0].shape[1]
     tall = round_up(height, 16)
     plain = pltpu.VMEM((across, height, channels), BF16)
     padded = pltpu.VMEM((across, tall, channels), BF16)
     rim = pltpu.VMEM((across + 2, tall, filters), F32)
-    shards = (square_shard, column_shard, older_shard)
+    pre = pltpu.VMEM((across, tall, filters), BF16)
     fulls = [(count * x.shape[0], x.shape[1]) for x in shards]
     anywhere = pl.BlockSpec(memory_space=pl.ANY)
     inside = pl.BlockSpec(memory_space=pltpu.VMEM)
     back = jax.ShapeDtypeStruct((across, tall, filters), BF16)
-    flops = 2 * across * tall * filters * (channels + 3 * filters)
     return pl.pallas_call(
         early_kernel,
         out_shape=[
             back,
             back,
-            jax.ShapeDtypeStruct((across, height, 2 * filters), BF16),
-            jax.ShapeDtypeStruct(fulls[0], BF16),
+            jax.ShapeDtypeStruct((across, height, 4 * filters), BF16),
             jax.ShapeDtypeStruct(fulls[2], BF16),
+            jax.ShapeDtypeStruct(fulls[3], BF16),
         ],
-        in_specs=[anywhere] * 5 + [inside] * 2,
-        out_specs=[inside] * 3 + [anywhere] * 2,
-        scratch_shapes=[plain, plain, padded, padded]
+        in_specs=[anywhere] * 7 + [inside] * 2,
+        out_specs=[anywhere] * 5,
+        scratch_shapes=[plain] * 3
+        + [padded] * 3
         + [pltpu.VMEM(shape, BF16) for shape in fulls]
         + [rim, rim, pltpu.VMEM((across, tall, filters), F32)]
-        + [pltpu.VMEM((across, tall, filters), BF16)]
-        + [pltpu.SemaphoreType.DMA((2,)), pltpu.SemaphoreType.DMA((2,))]
+        + [pre] * 4
+        + [pltpu.VMEM((across, height, 4 * filters), BF16)]
+        + [pltpu.SemaphoreType.DMA((3,)), pltpu.SemaphoreType.DMA((8,))]
         + exchange_semaphores(shards),
         compiler_params=pltpu.CompilerParams(
-            collective_id=0, has_side_effects=True, vmem_limit_bytes=48 * 1024 * 1024
+            collective_id=0, has_side_effects=True, vmem_limit_bytes=60 * 1024 * 1024
         ),
-        cost_estimate=pl.CostEstimate(flops=flops, bytes_accessed=20 * older.size, transcendentals=0),
         name="early",
-    )(older, grads, *shards, square_taps, column_taps)
+    )(older, newer, grads, *shards, square_taps, column_taps)
 
 
 def grad_blocks(back, full, pad, buf, hbm, sems, height):
@@ -492,8 +546,9 @@
         def grad_tile(at, base=q * filters):
             cols = pl.ds(pl.multiple_of(base + at, tile), tile)
             term = dot_turned(back[...].reshape(across * tall, filters), full[cols, :])
-            term = jnp.where(pad[:, :, cols] > 0, term.reshape(across, tall, tile), 0.0)
-            buf[:, :, cols] = term[:, :height].astype(BF16)
+            keep = pad[:, :, cols] > 0
+            term = term.reshape(across, tall, tile)[:, :height]
+            buf[:, :, cols] = jnp.where(keep, term, 0.0).astype(BF16)
 
         tiles(filters, tile, grad_tile)
         cols = pl.ds(q * filters, filters)
@@ -502,126 +557,75 @@
     return outs
 
 
-def older_kernel(older_hbm, back, full, out_hbm, older_in, pad, buf, in_sem, out_sems):
+def late_kernel(
+    older_hbm,
+    newer_hbm,
+    back_a_hbm,
+    back_b_hbm,
+    cell_in_hbm,
+    older_full_hbm,
+    newer_full_hbm,
+    cell_hbm,
+    older_out_hbm,
+    newer_out_hbm,
+    older_in,
+    newer_in,
+    back_a,
+    back_b,
+    older_full,
+    newer_full,
+    older_buf,
+    newer_buf,
+    in_sems,
+    cell_sem,
+    older_sems,
+    newer_sems,
+):
     height = older_in.shape[1]
-    load = pltpu.make_async_copy(older_hbm, older_in, in_sem)
-    load.start()
-    load.wait()
-    pad[:, :height, :] = older_in[...]
-    for copy in grad_blocks(back, full, pad, buf, out_hbm, out_sems, height):
+    loads = [
+        pltpu.make_async_copy(src, dst, in_sems.at[n])
+        for n, (src, dst) in enumerate(
+            (
+                (back_a_hbm, back_a),
+                (older_full_hbm, older_full),
+                (older_hbm, older_in),
+                (back_b_hbm, back_b),
+                (newer_full_hbm, newer_full),
+                (newer_hbm, newer_in),
+            )
+        )
+    ]
+    for copy in loads:
+        copy.start()
+    whole = pltpu.make_async_copy(cell_in_hbm, cell_hbm, cell_sem)
+    whole.start()
+    for copy in loads[:3]:
         copy.wait()
-
-
-def older_part(older, back, full):
-    across, height, channels = older.shape
-    tall, filters = back.shape[1:]
+    outs = grad_blocks(back_a, older_full, older_in, older_buf, older_out_hbm, older_sems, height)
+    for copy in loads[3:]:
+        copy.wait()
+    outs += grad_blocks(back_b, newer_full, newer_in, newer_buf, newer_out_hbm, newer_sems, height)
+    for copy in outs + [whole]:
+        copy.wait()
+
+
+def late(older, newer, back_a, back_b, cell, older_full, newer_full):
     plain = pltpu.VMEM(older.shape, BF16)
+    back = pltpu.VMEM(back_a.shape, BF16)
+    full = pltpu.VMEM(older_full.shape, BF16)
+    blocks = older_full.shape[0] // older_full.shape[1]
     anywhere = pl.BlockSpec(memory_space=pl.ANY)
-    inside = pl.BlockSpec(memory_space=pltpu.VMEM)
     return pl.pallas_call(
-        older_kernel,
-        out_shape=jax.ShapeDtypeStruct(older.shape, BF16),
-        in_specs=[anywhere, inside, inside],
-        out_specs=anywhere,
-        scratch_shapes=[plain, pltpu.VMEM((across, tall, channels), BF16), plain]
-        + [pltpu.SemaphoreType.DMA(()), pltpu.SemaphoreType.DMA((channels // filters,))],
-        compiler_params=pltpu.CompilerParams(vmem_limit_bytes=40 * 1024 * 1024),
-        cost_estimate=pl.CostEstimate(
-            flops=2 * across * tall * filters * channels, bytes_accessed=6 * older.size, transcendentals=0
-        ),
-        name="older",
-    )(older, back, full)
-
-
-def newer_kernel(
-    newer_hbm,
-    branch_hbm,
-    back,
-    newer_full,
-    square_full,
-    square_taps,
-    cell_hbm,
-    out_hbm,
-    newer_in,
-    pad,
-    buf,
-    cell_buf,
-    rim,
-    pre,
-    in_sems,
-    out_sems,
-    grad_sems,
-):
-    across, height, channels = newer_in.shape
-    tall = pad.shape[1]
-    filters = square_full.shape[0]
-    wide = across * tall
-    tile = min(filters, 256)
-    load = pltpu.make_async_copy(newer_hbm, newer_in, in_sems.at[0])
-    load.start()
-    middle = pl.ds(filters, 2 * filters)
-    fetch = pltpu.make_async_copy(branch_hbm, cell_buf.at[:, :, middle], in_sems.at[1])
-    fetch.start()
-    clear_ends(rim)
-    shift = make_shift(tall)
-    load.wait()
-    pad[:, :height, :] = jnp.maximum(newer_in[...], 0)
-    outs = grad_blocks(back, newer_full, pad, buf, out_hbm, grad_sems, height)
-    fetch.wait()
-
-    def send(columns, slot):
-        copy = pltpu.make_async_copy(cell_buf.at[:, :, columns], cell_hbm.at[:, :, columns], out_sems.at[slot])
-        copy.start()
-        outs.append(copy)
-
-    send(middle, 0)
-
-    def mix_tile(at):
-        cols = pl.ds(at, tile)
-        total = dot_rows(pad[...].reshape(wide, channels), newer_full[:, cols])
-        mixed = total.astype(BF16).reshape(across, tall, tile)
-        rim[1 : across + 1, :, cols] = mixed.astype(F32)
-        cell_buf[:, :, pl.ds(pl.multiple_of(3 * filters + at, tile), tile)] = mixed[:, :height]
-
-    tiles(filters, tile, mix_tile)
-    send(pl.ds(3 * filters, filters), 1)
-
-    def mix_plane(w, cols):
-        taps = tap_rows(square_taps, cols, 9)
-        total = square_sum(rim[w, :, cols], rim[w + 1, :, cols], rim[w + 2, :, cols], taps, False, shift)
-        pre[w, :, cols] = total.astype(BF16)
-
-    planes(0, filters // LANES, across, mix_plane)
-
-    def point_tile(at):
-        cols = pl.ds(at, tile)
-        term = dot_rows(pre[...].reshape(wide, filters), square_full[:, cols])
-        cell_buf[:, :, cols] = term.reshape(across, tall, tile)[:, :height].astype(BF16)
-
-    tiles(filters, tile, point_tile)
-    send(pl.ds(0, filters), 2)
-    for copy in outs:
-        copy.wait()
-
-
-def newer_part(newer, branch, back, newer_full, square_full, square_taps):
-    across, height, channels = newer.shape
-    tall, filters = back.shape[1:]
-    plain = pltpu.VMEM(newer.shape, BF16)
-    anywhere = pl.BlockSpec(memory_space=pl.ANY)
-    inside = pl.BlockSpec(memory_space=pltpu.VMEM)
-    return pl.pallas_call(
-        newer_kernel,
-        out_shape=[jax.ShapeDtypeStruct(newer.shape, BF16)] * 2,
-        in_specs=[anywhere] * 2 + [inside] * 4,
-        out_specs=[anywhere] * 2,
-        scratch_shapes=[plain, pltpu.VMEM((across, tall, channels), BF16), plain, plain]
-        + [pltpu.VMEM((across + 2, tall, filters), F32), pltpu.VMEM((across, tall, filters), BF16)]
-        + [pltpu.SemaphoreType.DMA((2,)), pltpu.SemaphoreType.DMA((3,))]
-        + [pltpu.SemaphoreType.DMA((channels // filters,))],
-        compiler_params=pltpu.CompilerParams(vmem_limit_bytes=48 * 1024 * 1024),
-        name="newer",
-    )(newer, branch, back, newer_full, square_full, square_taps)
+        late_kernel,
+        out_shape=[jax.ShapeDtypeStruct(x.shape, BF16) for x in (cell, older, newer)],
+        in_specs=[anywhere] * 7,
+        out_specs=[anywhere] * 3,
+        scratch_shapes=[plain, plain, back, back, full, full, plain, plain]
+        + [pltpu.SemaphoreType.DMA((6,)), pltpu.SemaphoreType.DMA(())]
+        + [pltpu.SemaphoreType.DMA((blocks,))] * 2,
+        compiler_params=pltpu.CompilerParams(vmem_limit_bytes=60 * 1024 * 1024),
+        name="late",
+    )(older, newer, back_a, back_b, cell, older_full, newer_full)
 
 
 def whole_images(
@@ -636,16 +640,21 @@
     column_kernel,
 ):
     count = lax.axis_size("rows")
-    filters = square_point.shape[1]
-    newer_full = lax.all_gather(newer_weight, "rows", axis=0, tiled=True)
     older, newer, grads = (jnp.transpose(x, (1, 0, 2)) for x in (older_output, newer_output, output_grad))
-    square_taps = square_kernel.reshape(9, filters)
-    back_a, back_b, branch, square_full, older_full = early(
-        older, grads, square_point, column_point, older_weight, square_taps, column_kernel, count
-    )
-    older_grad = older_part(older, back_a, older_full)
-    cell_output, newer_grad = newer_part(newer, branch, back_b, newer_full, square_full, square_taps)
-    return tuple(jnp.transpose(x, (1, 0, 2)) for x in (cell_output, older_grad, newer_grad))
+    outs = late(
+        older,
+        newer,
+        *early(
+            older,
+            newer,
+            grads,
+            (square_point, column_point, older_weight, newer_weight),
+            square_kernel.reshape(9, square_point.shape[1]),
+            column_kernel,
+            count,
+        ),
+    )
+    return tuple(jnp.transpose(x, (1, 0, 2)) for x in outs)
 
 
 def choose(*arrays):

time: 67.7 us -> 152 us (2.25)
  Pallas kernels: 45 us -> 150 us
  between operations: 14.1 us -> 0.64 us
  local copies, waits for them, and re-layouts: 7.48 us -> 1.36 us
    pallas_call x2 -> x1, Pallas kernels: 15.5 us -> 96.5 us  [late(): pl.pallas_call(late_kernel, out_shape=[jax.ShapeDtypeStruct(x.shape, BF16...]
    pallas_call x1, Pallas kernels: 29.5 us -> 53.2 us  [early(): pl.pallas_call(early_kernel, out_shape=[back, back, jax.ShapeDtypeStruct(...]
    unnamed x14 -> x0, local copies, waits for them, and re-layouts: 6.73 us -> none
  transfers between devices with their start and end apart: 1 -> 0, of which waited for: 0 -> 0; matrix products, arithmetic and copies ran while one was open for 1% -> 0% of each run, Pallas kernels for 51% -> 0%
where the time goes in v1:
time: 152 us
  Pallas kernels  150 us (99%)
    pallas_call x1, Pallas kernels, late(): pl.pallas_call(late_kernel, out_shape=[jax.ShapeDtypeStruct(x.shape, BF16...  96.5 us
    pallas_call x1, Pallas kernels, early(): pl.pallas_call(early_kernel, out_shape=[back, back, jax.ShapeDtypeStruct(...  53.2 us

profile of v1, /device:TPU:0, one launch (start us, length us, event | category | flops | bytes accessed | tf_op | source)
XLA Modules:
  0.0 151.7 jit_solution(17584493203611020886)
XLA Ops:
  0.6 1.4 reshape.9.square_taps
  2.0 53.2 %early.1 = (bf16[12,64,512]{2,1,0:T(8,128)(2,1)}, bf16[12,64,512]{2,1,0:T(8,128)(2,1)}, bf16[12,60,2048]{2,1,0:T(8,128)(2,1)}, bf16[2048,512]{1,0:T(8,128)(2,1)}, bf16[2048,512]{1,0:T(8,128)(2,1)}) custom-call(bf16[12,60,2048]{2,1,0:T(8,128)(2,1)} %bitcast.6, bf16[12,60,2048]{2,1,0:T(8,128)(2,1)} %bitcast.8, bf16[12,60,2048]{2,1,0:T(8,128)(2,1)} %bitcast.10, ...), custom_call_target="tpu_custom_call" | custom-call | tf_op jit(solution)/shard_map/early/pallas_call | solution.py:513
  55.2 96.5 %late.1 = (bf16[12,60,2048]{2,1,0:T(8,128)(2,1)}, bf16[12,60,2048]{2,1,0:T(8,128)(2,1)}, bf16[12,60,2048]{2,1,0:T(8,128)(2,1)}) custom-call(bf16[12,60,2048]{2,1,0:T(8,128)(2,1)} %bitcast.7, bf16[12,60,2048]{2,1,0:T(8,128)(2,1)} %bitcast.9, bf16[12,64,512]{2,1,0:T(8,128)(2,1)} %get-tuple-element.11.back_a_hbm, ...), custom_call_target="tpu_custom_call" | custom-call | tf_op jit(solution)/shard_map/late/pallas_call | solution.py:618

commit v2 on v1

--- a/solution.py
+++ b/solution.py
@@ -172,17 +172,26 @@
 
 
 class Exchange:
-    def __init__(self, shards, fulls, own_sem, y_sems, x_sems, side_sems):
+    def __init__(self, shards, fulls, own_sem, y_sems, x_sems, side_sems, pass_sems):
+        self.own = []
+        for index, shard in enumerate(shards):
+            depth = shard.shape[0]
+            home = pl.ds(pl.multiple_of(lax.axis_index("rows") * depth, 64), depth)
+            self.own.append(pltpu.make_async_copy(shard, fulls[index].at[home], own_sem.at[index]))
+            self.own[index].start()
         part, row = lax.axis_index("dp"), lax.axis_index("rows")
         side, across = row + 1 - 2 * (row % 2), (row + 2) % 4
-        corner = across + 1 - 2 * (across % 2)
         mate = part + 1 - 2 * (part % 2)
-        mine = part % 2
+        mine, theirs = part % 2, 1 - part % 2
         barrier = pltpu.get_barrier_semaphore()
-        for device in ((part, side), (part, across), (part, corner), (mate, row)):
+        for device in ((part, side), (part, across), (mate, row)):
             pl.semaphore_signal(barrier, inc=1, device_id=device, device_id_type=MESH)
-        pl.semaphore_wait(barrier, 4)
+        pl.semaphore_wait(barrier, 3)
         self.pieces = weight_pieces(shards)
+
+        def span(index, owner, half, at, rows):
+            depth = shards[index].shape[0]
+            return pl.ds(pl.multiple_of(owner * depth + half * (depth // 2) + at, 64), rows)
 
         def remote(src, dst, sems, slot, device):
             return pltpu.make_async_remote_copy(
@@ -194,55 +203,44 @@
                 device_id_type=MESH,
             )
 
-        self.y, self.x, self.own, self.side = [], [], [], []
+        self.y, self.x, self.low, self.high, self.side = [], [], [], [], []
+        total = len(self.pieces)
         for slot, (index, at, rows) in enumerate(self.pieces):
-            depth = shards[index].shape[0]
-            base = mine * (depth // 2) + at
-            start = shards[index].at[pl.ds(pl.multiple_of(base, 64), rows)]
-            sent, near, far = (
-                fulls[index].at[pl.ds(pl.multiple_of(owner * depth + base, 64), rows)]
-                for owner in (row, across, corner)
-            )
-            self.y.append(
-                [
-                    remote(start, sent, y_sems, 2 * slot, (part, across)),
-                    remote(start, sent, y_sems, 2 * slot + 1, (part, corner)),
-                ]
-            )
-            self.x.append(
-                [
-                    remote(near, near, x_sems, 2 * slot, (mate, row)),
-                    remote(far, far, x_sems, 2 * slot + 1, (mate, row)),
-                ]
-            )
+            sent = fulls[index].at[span(index, row, mine, at, rows)]
+            got = fulls[index].at[span(index, across, mine, at, rows)]
+            other = fulls[index].at[span(index, across, theirs, at, rows)]
+            self.y.append(remote(sent, sent, y_sems, slot, (part, across)))
+            self.x.append(remote(got, got, x_sems, slot, (mate, row)))
+            self.low.append(remote(got, got, pass_sems, slot, (part, side)))
+            self.high.append(remote(other, other, pass_sems, total + slot, (part, side)))
         for index, shard in enumerate(shards):
             depth = shard.shape[0]
             home = fulls[index].at[pl.ds(pl.multiple_of(row * depth, 64), depth)]
-            self.side.append(remote(shard, home, side_sems, index, (part, side)))
-            self.own.append(pltpu.make_async_copy(shard, home, own_sem.at[index]))
+            self.side.append(remote(home, home, side_sems, index, (part, side)))
         for index in range(len(shards)):
+            self.own[index].wait()
             for slot, piece in enumerate(self.pieces):
                 if piece[0] == index:
-                    self.y[slot][0].start()
-                    self.y[slot][1].start()
-            self.side[index].start()
-            self.own[index].start()
+                    self.y[slot].start()
 
     def forward(self, slot):
-        for come, go in zip(self.y[slot], self.x[slot]):
-            come.wait_recv()
-            go.start()
+        if slot < len(self.pieces):
+            self.y[slot].wait_recv()
+            self.x[slot].start()
+            self.low[slot].start()
+        if slot > 0:
+            self.x[slot - 1].wait_recv()
+            self.high[slot - 1].start()
 
     def wait_array(self, index):
         for slot, piece in enumerate(self.pieces):
             if piece[0] == index:
-                for copy in self.x[slot]:
-                    copy.wait_recv()
+                self.low[slot].wait_recv()
+                self.high[slot].wait_recv()
         self.side[index].wait_recv()
-        self.own[index].wait()
 
     def finish(self):
-        for copy in sum(self.y, []) + sum(self.x, []) + self.side:
+        for copy in self.y + self.x + self.low + self.high + self.side:
             copy.wait_send()
 
 
@@ -250,9 +248,10 @@
     total, number = len(weight_pieces(shards)), len(shards)
     return [
         pltpu.SemaphoreType.DMA((number,)),
+        pltpu.SemaphoreType.DMA((2, total)),
+        pltpu.SemaphoreType.DMA((2, total)),
+        pltpu.SemaphoreType.DMA((2, number)),
         pltpu.SemaphoreType.DMA((2, 2 * total)),
-        pltpu.SemaphoreType.DMA((2, 2 * total)),
-        pltpu.SemaphoreType.DMA((2, number)),
     ]
 
 
@@ -394,17 +393,21 @@
         cols = pl.ds(q * filters, filters)
         put(cell_buf.at[:, :, cols], cell_hbm.at[:, :, cols])
 
+    for index in range(3):
+        trade.side[index].start()
     clear_ends(rim_a)
     clear_ends(rim_b)
     shift = make_shift(tall)
     ins[0].wait()
     grads_pad[:, :height, :] = grads_in[...]
-    trade.forward(0)
-    trade.forward(1)
+    slots = [[n for n, piece in enumerate(trade.pieces) if piece[0] == index] for index in range(4)]
+    for slot in slots[0] + slots[1]:
+        trade.forward(slot)
     ins[1].wait()
     older_pad[:, :height, :] = jnp.maximum(older_in[...], 0)
     ins[2].wait()
     newer_pad[:, :height, :] = jnp.maximum(newer_in[...], 0)
+    trade.forward(slots[2][0])
     trade.wait_array(0)
     trade.wait_array(1)
 
@@ -428,14 +431,13 @@
         total = total + pool_sum(rim_b[w, :, cols], rim_b[w + 1, :, cols], rim_b[w + 2, :, cols], shift)
         back_a[w, :, cols] = total.astype(BF16)
 
-    older_slots = [n for n, piece in enumerate(trade.pieces) if piece[0] == 2]
-    newer_slots = [n for n, piece in enumerate(trade.pieces) if piece[0] == 3]
     done = 0
-    for n, slot in enumerate(older_slots):
-        until = (n + 1) * chunks // len(older_slots)
+    for n, slot in enumerate(slots[2]):
+        until = (n + 1) * chunks // len(slots[2])
         planes(done, until, across, back_plane)
         done = until
-        trade.forward(slot)
+        trade.forward(slot + 1)
+    trade.side[3].start()
     put(back_a, back_a_hbm)
     put(back_b, back_b_hbm)
     trade.wait_array(2)
@@ -456,9 +458,9 @@
         cell_buf[w, :, pool] = total[:height].astype(BF16)
 
     done = 0
-    for n, slot in enumerate(newer_slots):
-        trade.forward(slot)
-        until = (n + 1) * chunks // len(newer_slots)
+    for n, slot in enumerate(slots[3]):
+        trade.forward(slot + 1)
+        until = (n + 1) * chunks // len(slots[3])
         planes(done, until, across, older_plane)
         done = until
     put_block(2)
@@ -576,6 +578,7 @@
     newer_full,
     older_buf,
     newer_buf,
+    cell_buf,
     in_sems,
     cell_sem,
     older_sems,
@@ -592,18 +595,19 @@
                 (back_b_hbm, back_b),
                 (newer_full_hbm, newer_full),
                 (newer_hbm, newer_in),
+                (cell_in_hbm, cell_buf),
             )
         )
     ]
     for copy in loads:
         copy.start()
-    whole = pltpu.make_async_copy(cell_in_hbm, cell_hbm, cell_sem)
-    whole.start()
     for copy in loads[:3]:
         copy.wait()
     outs = grad_blocks(back_a, older_full, older_in, older_buf, older_out_hbm, older_sems, height)
     for copy in loads[3:]:
         copy.wait()
+    whole = pltpu.make_async_copy(cell_buf, cell_hbm, cell_sem)
+    whole.start()
     outs += grad_blocks(back_b, newer_full, newer_in, newer_buf, newer_out_hbm, newer_sems, height)
     for copy in outs + [whole]:
         copy.wait()
@@ -620,8 +624,8 @@
         out_shape=[jax.ShapeDtypeStruct(x.shape, BF16) for x in (cell, older, newer)],
         in_specs=[anywhere] * 7,
         out_specs=[anywhere] * 3,
-        scratch_shapes=[plain, plain, back, back, full, full, plain, plain]
-        + [pltpu.SemaphoreType.DMA((6,)), pltpu.SemaphoreType.DMA(())]
+        scratch_shapes=[plain, plain, back, back, full, full, plain, plain, plain]
+        + [pltpu.SemaphoreType.DMA((7,)), pltpu.SemaphoreType.DMA(())]
         + [pltpu.SemaphoreType.DMA((blocks,))] * 2,
         compiler_params=pltpu.CompilerParams(vmem_limit_bytes=60 * 1024 * 1024),
         name="late",

time: 152 us -> 50.4 us (0.33)
  Pallas kernels: 150 us -> 48.1 us
    pallas_call x1, Pallas kernels: 96.5 us -> 10.2 us  [late(): pl.pallas_call(late_kernel, out_shape=[jax.ShapeDtypeStruct(x.shape, BF16...]
    pallas_call x1, Pallas kernels: 53.2 us -> 37.9 us  [early(): pl.pallas_call(early_kernel, out_shape=[back, back, jax.ShapeDtypeStruct(...]
where the time goes in v2:
time: 50.4 us; the launch traced here: 50.1 us
  Pallas kernels  48.1 us (95%)
  local copies, waits for them, and re-layouts  1.36 us (3%)
  between operations  0.64 us (1%)
    pallas_call x1, Pallas kernels, early(): pl.pallas_call(early_kernel, out_shape=[back, back, jax.ShapeDtypeStruct(...  37.9 us
    pallas_call x1, Pallas kernels, late(): pl.pallas_call(late_kernel, out_shape=[jax.ShapeDtypeStruct(x.shape, BF16...  10.2 us
    reshape x1, local copies, waits for them, and re-layouts, whole_images(): square_kernel.reshape(9, square_point.shape[1])  1.36 us

profile of v2, /device:TPU:0, one launch (start us, length us, event | category | flops | bytes accessed | tf_op | source)
XLA Modules:
  0.0 50.1 jit_solution(8528018319098772663)
XLA Ops:
  0.6 1.4 %reshape.9.square_taps = f32[9,512]{1,0:T(8,128)} reshape(f32[3,3,512]{2,1,0:T(4,128)} %param.16) | data formatting | bytes 36864 | tf_op jit(solution)/shard_map/reshape | solution.py:656
  2.0 37.9 %early.1 = (bf16[12,64,512]{2,1,0:T(8,128)(2,1)}, bf16[12,64,512]{2,1,0:T(8,128)(2,1)}, bf16[12,60,2048]{2,1,0:T(8,128)(2,1)}, bf16[2048,512]{1,0:T(8,128)(2,1)}, bf16[2048,512]{1,0:T(8,128)(2,1)}) custom-call(bf16[12,60,2048]{2,1,0:T(8,128)(2,1)} %bitcast.6, bf16[12,60,2048]{2,1,0:T(8,128)(2,1)} %bitcast.8, bf16[12,60,2048]{2,1,0:T(8,128)(2,1)} %bitcast.10, ...), custom_call_target="tpu_custom_call" | custom-call | tf_op jit(solution)/shard_map/early/pallas_call | solution.py:515
  39.9 10.2 %late.1 = (bf16[12,60,2048]{2,1,0:T(8,128)(2,1)}, bf16[12,60,2048]{2,1,0:T(8,128)(2,1)}, bf16[12,60,2048]{2,1,0:T(8,128)(2,1)}) custom-call(bf16[12,60,2048]{2,1,0:T(8,128)(2,1)} %bitcast.7, bf16[12,60,2048]{2,1,0:T(8,128)(2,1)} %bitcast.9, bf16[12,64,512]{2,1,0:T(8,128)(2,1)} %get-tuple-element.11.back_a_hbm, ...), custom_call_target="tpu_custom_call" | custom-call | tf_op jit(solution)/shard_map/late/pallas_call | solution.py:622
